TPU v7x, 128 devices: a whole 4x4x4 slice. The times are simulated.
128 devices in a mesh: tm: 4 (over x), mesh: 32 (over y, z, core).
Axes of the slice: x: 4, y: 4, z: 4, core: 2. Of those that a mesh axis runs over, the one named last changes fastest.
Arguments:
- right_sides: bfloat16 [8, 4096, 512], P('tm', 'mesh'), may hold values from -6 to 6
- diag_inverse: bfloat16 [8, 4096, 4096], P('tm', 'mesh'), may hold values from -0.09375 to 0.09375
- coupling: bfloat16 [8, 4096, 4096], P('tm', 'mesh'), may hold values from -0.0625 to 0.0625
- carry_in: bfloat16 [4096, 512], P('mesh'), may hold values from -6 to 6
- arrow_blocks: bfloat16 [8, 64, 4096], P('tm', None, 'mesh'), may hold values from -0.03125 to 0.03125
- tip_right: float32 [64, 512], replicated, may hold values from -6 to 6
- tip_inverse: float32 [64, 64], replicated, may hold values from -0.75 to 0.75
Outputs:
- forward_state: bfloat16 [8, 4096, 512], P('tm', 'mesh')
- tip_solution: float32 [64, 512], replicated
All inputs are finite; a program needn't handle non-finite values.
Results may differ from a plain program's by a relative error of at most 0.011.
Values may be sent and summed in bfloat16 or wider, within the bound.
A program may use at most 64 MiB of HBM per device.

v0:
```python
import jax
import jax.numpy as jnp
from jax import lax
from jax.sharding import PartitionSpec as P


def from_behind(block, axis, distance):
    devices = range(lax.axis_size(axis))
    route = [(i - distance, i) for i in devices if i - distance in devices]
    return lax.ppermute(block, axis, route)


def advance(matrix, source, earlier):
    coupled = jnp.dot(
        matrix,
        lax.all_gather(earlier, "mesh", axis=0, tiled=True),
        preferred_element_type=jnp.float32,
    )
    return (source - coupled).astype(jnp.bfloat16)


def body(right_sides, diag_inverse, coupling, carry_in, arrow_blocks, tip_right, tip_inverse):
    position = lax.axis_index("tm")
    devices_tm = lax.axis_size("tm")
    blocks, own_rows, columns = right_sides.shape
    scaled = jnp.einsum(
        "tij,tjr->tir",
        diag_inverse,
        lax.all_gather(right_sides, "mesh", axis=1, tiled=True),
        preferred_element_type=jnp.float32,
    )
    incoming = carry_in
    outputs = []
    for wave_step in range(devices_tm):
        current = incoming
        outputs = []
        for block_no in range(blocks):
            current = advance(coupling[block_no], scaled[block_no], current)
            outputs.append(current)
        if wave_step + 1 < devices_tm:
            moved = from_behind(current, "tm", 1)
            incoming = jnp.where(position == 0, carry_in, moved)
    solved = jnp.stack(outputs, axis=0)
    arrow_terms = jnp.einsum(
        "tfr,trs->fs", arrow_blocks, solved, preferred_element_type=jnp.float32
    )
    arrow_sum = lax.psum(arrow_terms, ("tm", "mesh"))
    tip_solution = jnp.dot(
        tip_inverse,
        tip_right - arrow_sum,
        precision=lax.Precision.HIGHEST,
        preferred_element_type=jnp.float32,
    )
    return (solved, tip_solution)


def solution(mesh):
    placed = (
        P("tm", "mesh", None),
        P("tm", "mesh", None),
        P("tm", "mesh", None),
        P("mesh", None),
        P("tm", None, "mesh"),
        P(),
        P(),
    )
    return jax.shard_map(
        body, mesh=mesh, in_specs=placed, out_specs=(P("tm", "mesh", None), P()), check_vma=False
    )
```

profile of v0, /device:TPU:1, one launch (start us, length us, event | category | flops | bytes accessed | tf_op | source)
XLA Modules:
  0.0 639.1 jit_solution(520782583988940051)
XLA Ops:
  7.2 0.0 copy-start
  7.2 0.0 all-gather.10.cloned.1.call-start
  7.2 0.7 all-gather.10.cloned.1.call-update
  7.9 0.0 all-gather.12.cloned.1.call-start
  8.0 0.7 all-gather.12.cloned.1.call-update
  8.7 0.0 all-gather.14.cloned.1.call-start
  8.7 58.4 %all-gather.10.cloned.1.call-done = bf16[2,4096,512]{2,1,0:T(8,128)(2,1)} async-done(((bf16[2,128,512]{2,1,0:T(8,128)(2,1)}), bf16[2,4096,512]{2,1,0:T(8,128)(2,1)}) %all-gather.10.cloned.1.call-update) | async-done | bytes 8388624 | tf_op jit(solution)/shard_map/all_gather | solution.py:29
  67.1 0.0 copy-done
  67.1 4.6 fusion.33
  71.8 43.6 %all-gather.12.cloned.1.call-done = bf16[4096,512]{1,0:T(8,128)(2,1)} async-done(((bf16[128,512]{1,0:T(8,128)(2,1)}), bf16[4096,512]{1,0:T(8,128)(2,1)}) %all-gather.12.cloned.1.call-update) | async-done | bytes 4194320 | tf_op jit(solution)/shard_map/all_gather | solution.py:16
  115.3 3.9 fusion.7
  119.2 0.0 copy-start.1
  119.2 0.0 all-gather.14.cloned.1.call-update
  119.2 0.0 all-gather.16.cloned.1.call-start
  119.3 45.8 %all-gather.14.cloned.1.call-done = bf16[4096,512]{1,0:T(8,128)(2,1)} async-done(((bf16[128,512]{1,0:T(8,128)(2,1)}), bf16[4096,512]{1,0:T(8,128)(2,1)}) %all-gather.14.cloned.1.call-update) | async-done | bytes 4194320 | tf_op jit(solution)/shard_map/all_gather | solution.py:16
  165.1 3.2 fusion.14
  168.3 3.1 collective-permute-start
  171.4 2.6 collective-permute-done
  174.0 0.0 copy-done.1
  174.0 0.7 broadcast_select_fusion.2
  174.7 0.0 all-gather.16.cloned.1.call-update
  174.7 0.0 all-gather.18.cloned.1.call-start
  174.8 47.6 %all-gather.16.cloned.1.call-done = bf16[4096,512]{1,0:T(8,128)(2,1)} async-done(((bf16[128,512]{1,0:T(8,128)(2,1)}), bf16[4096,512]{1,0:T(8,128)(2,1)}) %all-gather.16.cloned.1.call-update) | async-done | bytes 4194320 | tf_op jit(solution)/shard_map/all_gather | solution.py:16
  222.4 3.9 fusion.13
  226.3 0.0 all-gather.18.cloned.1.call-update
  226.3 0.0 all-gather.20.cloned.1.call-start
  226.4 45.8 %all-gather.18.cloned.1.call-done = bf16[4096,512]{1,0:T(8,128)(2,1)} async-done(((bf16[128,512]{1,0:T(8,128)(2,1)}), bf16[4096,512]{1,0:T(8,128)(2,1)}) %all-gather.18.cloned.1.call-update) | async-done | bytes 4194320 | tf_op jit(solution)/shard_map/all_gather | solution.py:16
  272.2 3.2 fusion.12
  275.4 3.1 collective-permute-start.1
  278.5 2.6 collective-permute-done.1
  281.1 0.7 broadcast_select_fusion.1
  281.8 0.0 all-gather.20.cloned.1.call-update
  281.8 0.0 all-gather.22.cloned.1.call-start
  281.9 47.6 %all-gather.20.cloned.1.call-done = bf16[4096,512]{1,0:T(8,128)(2,1)} async-done(((bf16[128,512]{1,0:T(8,128)(2,1)}), bf16[4096,512]{1,0:T(8,128)(2,1)}) %all-gather.20.cloned.1.call-update) | async-done | bytes 4194320 | tf_op jit(solution)/shard_map/all_gather | solution.py:16
  329.5 3.9 fusion.11
  333.4 0.0 all-gather.22.cloned.1.call-update
  333.4 0.0 all-gather.24.cloned.1.call-start
  333.4 45.8 %all-gather.22.cloned.1.call-done = bf16[4096,512]{1,0:T(8,128)(2,1)} async-done(((bf16[128,512]{1,0:T(8,128)(2,1)}), bf16[4096,512]{1,0:T(8,128)(2,1)}) %all-gather.22.cloned.1.call-update) | async-done | bytes 4194320 | tf_op jit(solution)/shard_map/all_gather | solution.py:16
  379.2 3.2 fusion.10
  382.5 3.1 collective-permute-start.2
  385.6 2.6 collective-permute-done.2
  388.2 0.7 broadcast_select_fusion
  388.9 0.0 all-gather.24.cloned.1.call-update
  388.9 0.0 all-gather.26.cloned.1.call-start
  389.0 47.6 %all-gather.24.cloned.1.call-done = bf16[4096,512]{1,0:T(8,128)(2,1)} async-done(((bf16[128,512]{1,0:T(8,128)(2,1)}), bf16[4096,512]{1,0:T(8,128)(2,1)}) %all-gather.24.cloned.1.call-update) | async-done | bytes 4194320 | tf_op jit(solution)/shard_map/all_gather | solution.py:16
  436.6 3.9 fusion.9
  440.5 0.0 copy-start.2
  440.5 0.0 copy-start.5
  440.5 0.0 copy-start.4
  440.5 0.0 copy-start.6
  440.5 0.0 all-gather.26.cloned.1.call-update
  440.5 0.0 all-reduce.2.cloned.1.call-start
  440.6 45.8 %all-gather.26.cloned.1.call-done = bf16[4096,512]{1,0:T(8,128)(2,1)} async-done(((bf16[128,512]{1,0:T(8,128)(2,1)}), bf16[4096,512]{1,0:T(8,128)(2,1)}) %all-gather.26.cloned.1.call-update) | async-done | bytes 4194320 | tf_op jit(solution)/shard_map/all_gather | solution.py:16
  486.4 3.2 fusion.15
  489.6 0.0 copy-done.2
  489.6 0.0 copy-done.5
  489.6 0.0 copy-start.3
  489.7 0.8 convolution_bitcast_fusion.7
  490.5 0.0 all-reduce.2.cloned.1.call-update
  490.5 139.9 %all-reduce.2.cloned.1.call-done = f32[64,512]{1,0:T(8,128)} async-done(((f32[64,512]{1,0:T(8,128)}), f32[64,512]{1,0:T(8,128)}) %all-reduce.2.cloned.1.call-update) | async-done | bytes 131088 | tf_op jit(solution)/shard_map/psum | solution.py:47
  630.4 0.0 copy-done.4
  630.4 0.0 copy-done.6
  630.4 1.8 convolution_bitcast_fusion.8
  632.2 0.0 copy-done.3
  (1 shorter events, 0.0 us)
Async XLA Ops:
  7.2 60.0 %copy-start = (bf16[2,128,4096]{2,1,0:T(8,128)(2,1)S(1)}, bf16[2,128,4096]{2,1,0:T(8,128)(2,1)}, u32[]{:S(2)}) copy-start(bf16[2,128,4096]{2,1,0:T(8,128)(2,1)} %param.8) | copy-start | bytes 6291460
  7.2 59.9 %all-gather.10.cloned.1.call-start = ((), (), s32[]{:S(2)}) async-start(), calls=%async_computation | async-start | bytes 8650752 | tf_op jit(solution)/shard_map/all_gather | solution.py:29
  7.9 107.4 %all-gather.12.cloned.1.call-start = ((), (), s32[]{:S(2)}) async-start(), calls=%async_computation.1 | async-start | bytes 4325376 | tf_op jit(solution)/shard_map/all_gather | solution.py:16
  8.7 156.4 %all-gather.14.cloned.1.call-start = ((), (), s32[]{:S(2)}) async-start(), calls=%async_computation.2 | async-start | bytes 4325376 | tf_op jit(solution)/shard_map/all_gather | solution.py:16
  119.2 54.8 %copy-start.1 = (bf16[128,512]{1,0:T(8,128)(2,1)S(1)}, bf16[128,512]{1,0:T(8,128)(2,1)}, u32[]{:S(2)}) copy-start(bf16[128,512]{1,0:T(8,128)(2,1)} %param.10) | copy-start | bytes 393220
  119.2 103.2 %all-gather.16.cloned.1.call-start = ((), (), s32[]{:S(2)}) async-start(), calls=%async_computation.3 | async-start | bytes 4325376 | tf_op jit(solution)/shard_map/all_gather | solution.py:16
  168.3 5.7 collective-permute-start
  174.7 97.4 %all-gather.18.cloned.1.call-start = ((), (), s32[]{:S(2)}) async-start(), calls=%async_computation.4 | async-start | bytes 4325376 | tf_op jit(solution)/shard_map/all_gather | solution.py:16
  226.3 103.2 %all-gather.20.cloned.1.call-start = ((), (), s32[]{:S(2)}) async-start(), calls=%async_computation.5 | async-start | bytes 4325376 | tf_op jit(solution)/shard_map/all_gather | solution.py:16
  275.4 5.7 collective-permute-start.1
  281.8 97.4 %all-gather.22.cloned.1.call-start = ((), (), s32[]{:S(2)}) async-start(), calls=%async_computation.6 | async-start | bytes 4325376 | tf_op jit(solution)/shard_map/all_gather | solution.py:16
  333.4 103.2 %all-gather.24.cloned.1.call-start = ((), (), s32[]{:S(2)}) async-start(), calls=%async_computation.7 | async-start | bytes 4325376 | tf_op jit(solution)/shard_map/all_gather | solution.py:16
  382.5 5.7 collective-permute-start.2
  388.9 97.4 %all-gather.26.cloned.1.call-start = ((), (), s32[]{:S(2)}) async-start(), calls=%async_computation.8 | async-start | bytes 4325376 | tf_op jit(solution)/shard_map/all_gather | solution.py:16
  440.5 49.1 %copy-start.2 = (bf16[128,512]{1,0:T(8,128)(2,1)S(1)}, bf16[128,512]{1,0:T(8,128)(2,1)}, u32[]{:S(2)}) copy-start(bf16[128,512]{1,0:T(8,128)(2,1)} %fusion.9) | copy-start | bytes 393220
  440.5 49.2 %copy-start.5 = (bf16[2,64,128]{2,1,0:T(8,128)(2,1)S(1)}, bf16[2,64,128]{2,1,0:T(8,128)(2,1)}, u32[]{:S(2)}) copy-start(bf16[2,64,128]{2,1,0:T(8,128)(2,1)} %param.11) | copy-start | bytes 98308
  440.5 189.9 %copy-start.4 = (f32[64,512]{1,0:T(8,128)S(1)}, f32[64,512]{1,0:T(8,128)}, u32[]{:S(2)}) copy-start(f32[64,512]{1,0:T(8,128)} %param.12) | copy-start | bytes 393220
  440.5 189.9 %copy-start.6 = (f32[64,64]{1,0:T(8,128)S(1)}, f32[64,64]{1,0:T(8,128)}, u32[]{:S(2)}) copy-start(f32[64,64]{1,0:T(8,128)} %param.13) | copy-start | bytes 49156
  440.5 189.9 %all-reduce.2.cloned.1.call-start = ((), (), s32[]{:S(2)}) async-start(), calls=%async_computation.9 | async-start | bytes 262144 | tf_op jit(solution)/shard_map/psum | solution.py:47
  489.6 142.6 %copy-start.3 = (bf16[2,128,512]{2,1,0:T(8,128)(2,1)}, bf16[2,128,512]{2,1,0:T(8,128)(2,1)S(1)}, u32[]{:S(2)}) copy-start(bf16[2,128,512]{2,1,0:T(8,128)(2,1)S(1)} %pad_maximum_fusion) | copy-start | bytes 786436
Sparse Core Ops, SparseCore 0:
  10.4 56.6 all-gather.9
  69.4 45.8 all-gather.11
  119.4 45.6 all-gather.13
  174.8 47.5 all-gather.15
  226.4 45.6 all-gather.17
  281.9 47.4 all-gather.19
  333.5 45.6 all-gather.21
  389.0 47.5 all-gather.23
  440.6 45.6 all-gather.25
  491.5 138.8 all-reduce.1
where the time goes:
time: 639 us
  waiting for transfers between devices  577 us (90%)
  matrix products  35.8 us (6%)
  between operations  14.3 us (2%)
  starting transfers between devices  9.72 us (2%)
    all_gather x8, waiting for transfers between devices, advance(): lax.all_gather(earlier, 'mesh', axis=0, tiled=True)  370 us
    psum x1, waiting for transfers between devices, body(): arrow_sum = lax.psum(arrow_terms, ('tm', 'mesh'))  140 us
    all_gather x1, waiting for transfers between devices, body(): lax.all_gather(right_sides, 'mesh', axis=1, tiled=True)  58.4 us
    dot_general x8, matrix products, advance(): jnp.dot(matrix, lax.all_gather(earlier, 'mesh', axis=0, tiled=True), pref...  28.5 us
  transfers between devices with their start and end apart: 13, of which 13 were waited for; matrix products, arithmetic and copies ran while one was open for 1% of the time, Pallas kernels for 0%

commit v1 on v0

--- a/solution.py
+++ b/solution.py
@@ -44,7 +44,7 @@
     arrow_terms = jnp.einsum(
         "tfr,trs->fs", arrow_blocks, solved, preferred_element_type=jnp.float32
     )
-    arrow_sum = lax.psum(arrow_terms, ("tm", "mesh"))
+    arrow_sum = jnp.sum(lax.all_gather(arrow_terms, ("tm", "mesh")), axis=0)
     tip_solution = jnp.dot(
         tip_inverse,
         tip_right - arrow_sum,

time: 639 us -> 586 us (0.917)
  waiting for transfers between devices: 577 us -> 517 us
  other arithmetic: 2.05 us -> 9.2 us
    psum x1 -> x0, waiting for transfers between devices: 140 us -> none  [body(): arrow_sum = lax.psum(arrow_terms, ('tm', 'mesh'))]
    all_gather x0 -> x1, waiting for transfers between devices: none -> 79.8 us  [body(): arrow_sum = jnp.sum(lax.all_gather(arrow_terms, ('tm', 'mesh')), axis=0)]
    reduce_sum x0 -> x1, other arithmetic: none -> 7.15 us  [body(): arrow_sum = jnp.sum(lax.all_gather(arrow_terms, ('tm', 'mesh')), axis=0)]
where the time goes in v1:
time: 586 us; the launch traced here: 585 us
  waiting for transfers between devices  517 us (88%)
  matrix products  34.9 us (6%)
  between operations  14.3 us (2%)
  starting transfers between devices  9.72 us (2%)
  other arithmetic  9.2 us (2%)
    all_gather x8, waiting for transfers between devices, advance(): lax.all_gather(earlier, 'mesh', axis=0, tiled=True)  370 us
    all_gather x1, waiting for transfers between devices, body(): arrow_sum = jnp.sum(lax.all_gather(arrow_terms, ('tm', 'mesh')), axis=0)  79.8 us
    all_gather x1, waiting for transfers between devices, body(): lax.all_gather(right_sides, 'mesh', axis=1, tiled=True)  58.4 us
    dot_general x8, matrix products, advance(): jnp.dot(matrix, lax.all_gather(earlier, 'mesh', axis=0, tiled=True), pref...  28.5 us
  transfers between devices with their start and end apart: 13, of which 13 were waited for; matrix products, arithmetic and copies ran while one was open for 1% of the time, Pallas kernels for 0%

profile of v1, /device:TPU:1, one launch (start us, length us, event | category | flops | bytes accessed | tf_op | source)
XLA Modules:
  0.0 585.2 jit_solution(5920308752114790513)
XLA Ops:
  7.2 0.0 copy-start
  7.2 0.0 all-gather.12.cloned.1.call-start
  7.2 0.7 all-gather.12.cloned.1.call-update
  7.9 0.0 all-gather.14.cloned.1.call-start
  8.0 0.7 all-gather.14.cloned.1.call-update
  8.7 0.0 all-gather.16.cloned.1.call-start
  8.7 58.4 %all-gather.12.cloned.1.call-done = bf16[2,4096,512]{2,1,0:T(8,128)(2,1)} async-done(((bf16[2,128,512]{2,1,0:T(8,128)(2,1)}), bf16[2,4096,512]{2,1,0:T(8,128)(2,1)}) %all-gather.12.cloned.1.call-update) | async-done | bytes 8388624 | tf_op jit(solution)/shard_map/all_gather | solution.py:29
  67.1 0.0 copy-done
  67.1 4.6 fusion.33
  71.8 43.6 %all-gather.14.cloned.1.call-done = bf16[4096,512]{1,0:T(8,128)(2,1)} async-done(((bf16[128,512]{1,0:T(8,128)(2,1)}), bf16[4096,512]{1,0:T(8,128)(2,1)}) %all-gather.14.cloned.1.call-update) | async-done | bytes 4194320 | tf_op jit(solution)/shard_map/all_gather | solution.py:16
  115.3 3.9 fusion.7
  119.2 0.0 copy-start.1
  119.2 0.0 all-gather.16.cloned.1.call-update
  119.2 0.0 all-gather.18.cloned.1.call-start
  119.3 45.8 %all-gather.16.cloned.1.call-done = bf16[4096,512]{1,0:T(8,128)(2,1)} async-done(((bf16[128,512]{1,0:T(8,128)(2,1)}), bf16[4096,512]{1,0:T(8,128)(2,1)}) %all-gather.16.cloned.1.call-update) | async-done | bytes 4194320 | tf_op jit(solution)/shard_map/all_gather | solution.py:16
  165.1 3.2 fusion.14
  168.3 3.1 collective-permute-start
  171.4 2.6 collective-permute-done
  174.0 0.0 copy-done.1
  174.0 0.7 broadcast_select_fusion.2
  174.7 0.0 all-gather.18.cloned.1.call-update
  174.7 0.0 all-gather.20.cloned.1.call-start
  174.8 47.6 %all-gather.18.cloned.1.call-done = bf16[4096,512]{1,0:T(8,128)(2,1)} async-done(((bf16[128,512]{1,0:T(8,128)(2,1)}), bf16[4096,512]{1,0:T(8,128)(2,1)}) %all-gather.18.cloned.1.call-update) | async-done | bytes 4194320 | tf_op jit(solution)/shard_map/all_gather | solution.py:16
  222.4 3.9 fusion.13
  226.3 0.0 all-gather.20.cloned.1.call-update
  226.3 0.0 all-gather.22.cloned.1.call-start
  226.4 45.8 %all-gather.20.cloned.1.call-done = bf16[4096,512]{1,0:T(8,128)(2,1)} async-done(((bf16[128,512]{1,0:T(8,128)(2,1)}), bf16[4096,512]{1,0:T(8,128)(2,1)}) %all-gather.20.cloned.1.call-update) | async-done | bytes 4194320 | tf_op jit(solution)/shard_map/all_gather | solution.py:16
  272.2 3.2 fusion.12
  275.4 3.1 collective-permute-start.1
  278.5 2.6 collective-permute-done.1
  281.1 0.7 broadcast_select_fusion.1
  281.8 0.0 all-gather.22.cloned.1.call-update
  281.8 0.0 all-gather.24.cloned.1.call-start
  281.9 47.6 %all-gather.22.cloned.1.call-done = bf16[4096,512]{1,0:T(8,128)(2,1)} async-done(((bf16[128,512]{1,0:T(8,128)(2,1)}), bf16[4096,512]{1,0:T(8,128)(2,1)}) %all-gather.22.cloned.1.call-update) | async-done | bytes 4194320 | tf_op jit(solution)/shard_map/all_gather | solution.py:16
  329.5 3.9 fusion.11
  333.4 0.0 all-gather.24.cloned.1.call-update
  333.4 0.0 all-gather.26.cloned.1.call-start
  333.4 45.8 %all-gather.24.cloned.1.call-done = bf16[4096,512]{1,0:T(8,128)(2,1)} async-done(((bf16[128,512]{1,0:T(8,128)(2,1)}), bf16[4096,512]{1,0:T(8,128)(2,1)}) %all-gather.24.cloned.1.call-update) | async-done | bytes 4194320 | tf_op jit(solution)/shard_map/all_gather | solution.py:16
  379.2 3.2 fusion.10
  382.5 3.1 collective-permute-start.2
  385.6 2.6 collective-permute-done.2
  388.2 0.7 broadcast_select_fusion
  388.9 0.0 all-gather.26.cloned.1.call-update
  388.9 0.0 all-gather.28.cloned.1.call-start
  389.0 47.6 %all-gather.26.cloned.1.call-done = bf16[4096,512]{1,0:T(8,128)(2,1)} async-done(((bf16[128,512]{1,0:T(8,128)(2,1)}), bf16[4096,512]{1,0:T(8,128)(2,1)}) %all-gather.26.cloned.1.call-update) | async-done | bytes 4194320 | tf_op jit(solution)/shard_map/all_gather | solution.py:16
  436.6 3.9 fusion.9
  440.5 0.0 copy-start.2
  440.5 0.0 copy-start.5
  440.5 0.0 all-gather.28.cloned.1.call-update
  440.5 0.0 all-gather.30.cloned.1.call-start
  440.5 45.8 %all-gather.28.cloned.1.call-done = bf16[4096,512]{1,0:T(8,128)(2,1)} async-done(((bf16[128,512]{1,0:T(8,128)(2,1)}), bf16[4096,512]{1,0:T(8,128)(2,1)}) %all-gather.28.cloned.1.call-update) | async-done | bytes 4194320 | tf_op jit(solution)/shard_map/all_gather | solution.py:16
  486.3 3.2 fusion.15
  489.6 0.0 copy-done.2
  489.6 0.0 copy-done.5
  489.6 0.0 copy-start.3
  489.6 0.8 convolution_bitcast_fusion.7
  490.5 0.0 all-gather.30.cloned.1.call-update
  490.5 79.8 %all-gather.30.cloned.1.call-done = f32[8192,512]{1,0:T(8,128)} async-done(((f32[64,512]{1,0:T(8,128)}), f32[8192,512]{1,0:T(8,128)}) %all-gather.30.cloned.1.call-update) | async-done | bytes 16777232 | tf_op jit(solution)/shard_map/all_gather | solution.py:47
  570.3 0.0 copy-start.4
  570.3 7.2 %reduce_sum.9 = f32[64,512]{1,0:T(8,128)S(1)} reduce(f32[128,64,512]{2,1,0:T(8,128)} %bitcast.105, f32[]{:T(128)} %constant.9.clone.1), dimensions={0}, to_apply=%region_0.1 | reduce | flops 4161536 | bytes 16908292 | tf_op jit(solution)/shard_map/reduce_sum | solution.py:47
  577.4 0.0 copy-done.3
  577.4 0.0 copy-done.4
  577.4 0.0 copy-done.6
  577.4 0.9 convolution_bitcast_fusion.8
  (2 shorter events, 0.0 us)
Async XLA Ops:
  7.2 60.0 %copy-start = (bf16[2,128,4096]{2,1,0:T(8,128)(2,1)S(1)}, bf16[2,128,4096]{2,1,0:T(8,128)(2,1)}, u32[]{:S(2)}) copy-start(bf16[2,128,4096]{2,1,0:T(8,128)(2,1)} %param.8) | copy-start | bytes 6291460
  7.2 59.9 %all-gather.12.cloned.1.call-start = ((), (), s32[]{:S(2)}) async-start(), calls=%async_computation | async-start | bytes 8650752 | tf_op jit(solution)/shard_map/all_gather | solution.py:29
  7.9 107.4 %all-gather.14.cloned.1.call-start = ((), (), s32[]{:S(2)}) async-start(), calls=%async_computation.1 | async-start | bytes 4325376 | tf_op jit(solution)/shard_map/all_gather | solution.py:16
  8.7 156.4 %all-gather.16.cloned.1.call-start = ((), (), s32[]{:S(2)}) async-start(), calls=%async_computation.2 | async-start | bytes 4325376 | tf_op jit(solution)/shard_map/all_gather | solution.py:16
  119.2 54.8 %copy-start.1 = (bf16[128,512]{1,0:T(8,128)(2,1)S(1)}, bf16[128,512]{1,0:T(8,128)(2,1)}, u32[]{:S(2)}) copy-start(bf16[128,512]{1,0:T(8,128)(2,1)} %param.10) | copy-start | bytes 393220
  119.2 103.2 %all-gather.18.cloned.1.call-start = ((), (), s32[]{:S(2)}) async-start(), calls=%async_computation.3 | async-start | bytes 4325376 | tf_op jit(solution)/shard_map/all_gather | solution.py:16
  168.3 5.7 collective-permute-start
  174.7 97.4 %all-gather.20.cloned.1.call-start = ((), (), s32[]{:S(2)}) async-start(), calls=%async_computation.4 | async-start | bytes 4325376 | tf_op jit(solution)/shard_map/all_gather | solution.py:16
  226.3 103.2 %all-gather.22.cloned.1.call-start = ((), (), s32[]{:S(2)}) async-start(), calls=%async_computation.5 | async-start | bytes 4325376 | tf_op jit(solution)/shard_map/all_gather | solution.py:16
  275.4 5.7 collective-permute-start.1
  281.8 97.4 %all-gather.24.cloned.1.call-start = ((), (), s32[]{:S(2)}) async-start(), calls=%async_computation.6 | async-start | bytes 4325376 | tf_op jit(solution)/shard_map/all_gather | solution.py:16
  333.4 103.2 %all-gather.26.cloned.1.call-start = ((), (), s32[]{:S(2)}) async-start(), calls=%async_computation.7 | async-start | bytes 4325376 | tf_op jit(solution)/shard_map/all_gather | solution.py:16
  382.5 5.7 collective-permute-start.2
  388.9 97.4 %all-gather.28.cloned.1.call-start = ((), (), s32[]{:S(2)}) async-start(), calls=%async_computation.8 | async-start | bytes 4325376 | tf_op jit(solution)/shard_map/all_gather | solution.py:16
  440.5 49.1 %copy-start.2 = (bf16[128,512]{1,0:T(8,128)(2,1)S(1)}, bf16[128,512]{1,0:T(8,128)(2,1)}, u32[]{:S(2)}) copy-start(bf16[128,512]{1,0:T(8,128)(2,1)} %fusion.9) | copy-start | bytes 393220
  440.5 49.2 %copy-start.5 = (bf16[2,64,128]{2,1,0:T(8,128)(2,1)S(1)}, bf16[2,64,128]{2,1,0:T(8,128)(2,1)}, u32[]{:S(2)}) copy-start(bf16[2,64,128]{2,1,0:T(8,128)(2,1)} %param.11) | copy-start | bytes 98308
  440.5 129.8 %all-gather.30.cloned.1.call-start = ((), (), s32[]{:S(2)}) async-start(), calls=%async_computation.9 | async-start | bytes 16908288 | tf_op jit(solution)/shard_map/all_gather | solution.py:47
  489.6 87.8 %copy-start.3 = (bf16[2,128,512]{2,1,0:T(8,128)(2,1)}, bf16[2,128,512]{2,1,0:T(8,128)(2,1)S(1)}, u32[]{:S(2)}) copy-start(bf16[2,128,512]{2,1,0:T(8,128)(2,1)S(1)} %pad_maximum_fusion) | copy-start | bytes 786436
  570.3 7.2 %copy-start.4 = (f32[64,512]{1,0:T(8,128)S(1)}, f32[64,512]{1,0:T(8,128)}, u32[]{:S(2)}) copy-start(f32[64,512]{1,0:T(8,128)} %param.12) | copy-start | bytes 393220
  570.3 7.2 %copy-start.6 = (f32[64,64]{1,0:T(8,128)S(1)}, f32[64,64]{1,0:T(8,128)}, u32[]{:S(2)}) copy-start(f32[64,64]{1,0:T(8,128)} %param.13) | copy-start | bytes 49156
Sparse Core Ops, SparseCore 0:
  10.4 56.6 all-gather.11
  69.4 45.8 all-gather.13
  119.4 45.6 all-gather.15
  174.8 47.5 all-gather.17
  226.4 45.6 all-gather.19
  281.9 47.4 all-gather.21
  333.5 45.6 all-gather.23
  389.0 47.5 all-gather.25
  440.6 45.6 all-gather.27
  490.6 79.5 all-gather.29
